TPU v7x, 512 devices: a whole 4x8x8 slice. The times are simulated.
512 devices in a mesh: row: 8 (over z), col: 16 (over y, core), layer: 4 (over x).
Axes of the slice: x: 4, y: 8, z: 8, core: 2. Of those that a mesh axis runs over, the one named last changes fastest.
Arguments:
- panel_values: bfloat16 [16384, 8192], P('row', ('layer', 'col')), may hold values from -6 to 6
- slab_values: bfloat16 [8192, 6144], P(('layer', 'row'), 'col'), may hold values from -0.09375 to 0.09375
- pattern_panel: int32 [128, 64], P('row', ('layer', 'col')), may hold values from 0 to 1, as said below
- pattern_result: int32 [128, 48], P(('row', 'layer'), 'col'), may hold values 0 or 1
Outputs:
- product_slab: bfloat16 [16384, 6144], P(('row', 'layer'), 'col')
Inputs may be any that keep to these rules, and one draw needn't show every extreme that they name: `pattern_panel`: in every group of 16 blocks that one device holds of one block column (block rows r * 16 to r * 16 + 15), 1 to 8 are 1; some group reaches this bound: every group of block column 0 has exactly 8.
All inputs are finite; a program needn't handle non-finite values. No bound on the sum of `pattern_result` on one device may be relied on, other than what follows from the above.
Results may differ from a plain program's by a relative error of at most 0.001.
Values may be sent and summed in bfloat16 or wider, within the bound.
A program may use at most 64 MiB of HBM per device.

v0:
```python
import jax
import jax.numpy as jnp
from jax import lax
from jax.sharding import PartitionSpec as P


def per_device(panel_values, slab_values, pattern_panel, pattern_result):
    block = panel_values.shape[1]
    row_blocks = pattern_panel.shape[0]
    gathered = lax.all_gather(slab_values, "row", axis=0, tiled=True)
    flags = pattern_panel[:, 0]
    blocks_here = panel_values.reshape(row_blocks, block, block)
    masked = (blocks_here * flags.astype(jnp.bfloat16)[:, None, None]).reshape(
        row_blocks * block, block
    )
    partial_value = jnp.dot(
        lax.all_gather(masked, "col", axis=1, tiled=True),
        gathered,
        preferred_element_type=jnp.float32,
    )
    shares = lax.psum_scatter(partial_value, "layer", scatter_dimension=0, tiled=True)
    out_blocks = pattern_result.shape[0]
    col_blocks = pattern_result.shape[1]
    keeper = pattern_result.astype(jnp.float32)
    filtered = shares.reshape(out_blocks, block, col_blocks, block) * keeper[:, None, :, None]
    return filtered.reshape(shares.shape).astype(jnp.bfloat16)


def solution(mesh):
    placed = (
        P("row", ("layer", "col")),
        P(("layer", "row"), "col"),
        P("row", ("layer", "col")),
        P(("row", "layer"), "col"),
    )
    return jax.shard_map(
        per_device,
        mesh=mesh,
        in_specs=placed,
        out_specs=P(("row", "layer"), "col"),
        check_vma=False,
    )
```

profile of v0, /device:TPU:1, one launch (start us, length us, event | category | flops | bytes accessed | tf_op | source)
XLA Modules:
  0.0 186.3 jit_solution(16902584694863488766)
XLA Ops:
  6.5 0.0 all-gather.5.cloned.1.call-start
  6.5 0.7 all-gather.5.cloned.1.call-update
  7.3 0.0 all-gather.3.cloned.1.call-start
  7.3 0.7 convert_bitcast_fusion
  8.0 0.1 broadcast_bitcast_fusion
  8.0 2.2 %broadcast_multiply_fusion = bf16[2048,128]{1,0:T(8,128)(2,1)} fusion(bf16[2048,128]{1,0:T(8,128)(2,1)} %param.4, bf16[2048]{0:T(1024)(128)(2,1)S(1)} %broadcast_bitcast_fusion), kind=kLoop, calls=%fused_computation.2 | loop fusion | flops 262144 | bytes 1052672 | tf_op jit(solution)/shard_map/mul | solution.py:13
  10.3 0.0 all-gather.3.cloned.1.call-update
  10.3 0.0 reduce-scatter.2.cloned.1.call-start
  10.3 44.2 %all-gather.5.cloned.1.call-done = bf16[2048,384]{1,0:T(8,128)(2,1)} async-done(((bf16[256,384]{1,0:T(8,128)(2,1)}), bf16[2048,384]{1,0:T(8,128)(2,1)}) %all-gather.5.cloned.1.call-update) | async-done | bytes 1572880 | tf_op jit(solution)/shard_map/all_gather | solution.py:10
  54.5 73.2 %all-gather.3.cloned.1.call-done = bf16[2048,2048]{1,0:T(8,128)(2,1)} async-done(((bf16[2048,128]{1,0:T(8,128)(2,1)}), bf16[2048,2048]{1,0:T(8,128)(2,1)}) %all-gather.3.cloned.1.call-update) | async-done | bytes 8388624 | tf_op jit(solution)/shard_map/all_gather | solution.py:17
  127.7 10.1 %fusion = f32[2048,384]{1,0:T(8,128)} fusion(bf16[2048,2048]{1,0:T(8,128)(2,1)} %all-gather.3.cloned.1.call-done, bf16[2048,384]{1,0:T(8,128)(2,1)} %all-gather.5.cloned.1.call-done), kind=kOutput, calls=%fused_computation.5 | convolution fusion | flops 3221225472 | bytes 13107200 | tf_op jit(solution)/shard_map/dot_general | solution.py:16
  137.8 0.0 copy-start
  137.8 0.0 reduce-scatter.2.cloned.1.call-update
  137.8 0.7 copy-done
  138.4 0.1 copy.5
  138.5 0.2 mul.28
  138.7 0.1 copy.9
  138.8 0.3 copy.6
  139.1 38.8 %reduce-scatter.2.cloned.1.call-done = f32[512,384]{1,0:T(8,128)} async-done(((f32[2048,384]{1,0:T(8,128)}), f32[512,384]{1,0:T(8,128)}) %reduce-scatter.2.cloned.1.call-update) | async-done | bytes 786448 | tf_op jit(solution)/shard_map/reduce_scatter | solution.py:21
  177.8 2.0 %multiply_convert_fusion = bf16[512,384]{1,0:T(8,128)(2,1)} fusion(f32[512,384]{1,0:T(8,128)} %reduce-scatter.2.cloned.1.call-done, f32[512,384]{1,0:T(8,128)S(1)} %copy.6), kind=kLoop, calls=%fused_computation.1 | loop fusion | flops 393216 | bytes 1966080 | tf_op jit(solution)/shard_map/convert_element_type | solution.py:26
  (1 shorter events, 0.0 us)
Async XLA Ops:
  6.5 48.0 %all-gather.5.cloned.1.call-start = ((), (), s32[]{:S(2)}) async-start(), calls=%async_computation.2 | async-start | bytes 1769472 | tf_op jit(solution)/shard_map/all_gather | solution.py:10
  7.3 120.5 %all-gather.3.cloned.1.call-start = ((), (), s32[]{:S(2)}) async-start(), calls=%async_computation.1 | async-start | bytes 8912896 | tf_op jit(solution)/shard_map/all_gather | solution.py:17
  10.3 167.5 %reduce-scatter.2.cloned.1.call-start = ((), (), s32[]{:S(2)}) async-start(), calls=%async_computation.3 | async-start | bytes 3932160 | tf_op jit(solution)/shard_map/reduce_scatter | solution.py:21
  137.8 0.7 copy-start
Sparse Core Ops, SparseCore 0:
  9.4 45.0 all-gather.4
  56.6 71.0 all-gather.2
  137.9 39.8 reduce-scatter.1
where the time goes:
time: 187 us; the launch traced here: 186 us
  waiting for transfers between devices  157 us (84%)
  between operations  13.1 us (7%)
  matrix products  10.1 us (5%)
  other arithmetic  4.83 us (3%)
    all_gather x1, waiting for transfers between devices, per_device(): lax.all_gather(masked, 'col', axis=1, tiled=True)  73.2 us
    all_gather x1, waiting for transfers between devices, per_device(): gathered = lax.all_gather(slab_values, 'row', axis=0, tiled=True)  44.2 us
    reduce_scatter x1, waiting for transfers between devices, per_device(): lax.psum_scatter(partial_value, 'layer', scatter_dimension=0, tiled=True)  38.8 us
    dot_general x1, matrix products, per_device(): jnp.dot(lax.all_gather(masked, 'col', axis=1, tiled=True), gathered, pref...  10.1 us
  transfers between devices with their start and end apart: 3, of which 3 were waited for; matrix products, arithmetic and copies ran while one was open for 2% of the time, Pallas kernels for 0%

commit v1 on v0

--- a/solution.py
+++ b/solution.py
@@ -2,9 +2,20 @@
 import jax.numpy as jnp
 from jax import lax
 from jax.sharding import PartitionSpec as P
+from jax.lax import all_to_all, axis_size
 
 
 def per_device(panel_values, slab_values, pattern_panel, pattern_result):
+
+    def fit_the_pipes(at_axis, here_x):
+        tile_out = all_to_all(
+            jnp.stack([here_x for _ in range(axis_size("col"))]),
+            axis_name="col",
+            split_axis=0,
+            concat_axis=0,
+        )
+        return jnp.concatenate(tile_out, axis=at_axis)
+
     block = panel_values.shape[1]
     row_blocks = pattern_panel.shape[0]
     gathered = lax.all_gather(slab_values, "row", axis=0, tiled=True)
@@ -13,11 +24,7 @@
     masked = (blocks_here * flags.astype(jnp.bfloat16)[:, None, None]).reshape(
         row_blocks * block, block
     )
-    partial_value = jnp.dot(
-        lax.all_gather(masked, "col", axis=1, tiled=True),
-        gathered,
-        preferred_element_type=jnp.float32,
-    )
+    partial_value = jnp.dot(fit_the_pipes(1, masked), gathered, preferred_element_type=jnp.float32)
     shares = lax.psum_scatter(partial_value, "layer", scatter_dimension=0, tiled=True)
     out_blocks = pattern_result.shape[0]
     col_blocks = pattern_result.shape[1]

time: 187 us -> 271 us (1.45)
  waiting for transfers between devices: 157 us -> 226 us
  starting transfers between devices: 0.08 us -> 11.4 us
  local copies, waits for them, and re-layouts: 1.31 us -> 5.85 us
    all_to_all x0 -> x1, waiting for transfers between devices: none -> 140 us  [fit_the_pipes(): all_to_all(jnp.stack([here_x for _ in range(axis_size('col'))]), axis_nam...]
    all_gather x1 -> x0, waiting for transfers between devices: 73.2 us -> none  [per_device(): lax.all_gather(masked, 'col', axis=1, tiled=True)]
    all_to_all x0 -> x1, starting transfers between devices: none -> 11.3 us  [fit_the_pipes(): all_to_all(jnp.stack([here_x for _ in range(axis_size('col'))]), axis_nam...]
    another operation x0 -> x1, local copies, waits for them, and re-layouts: none -> 4.32 us  [fit_the_pipes(): jnp.stack([here_x for _ in range(axis_size('col'))])]
    reduce_scatter x1, waiting for transfers between devices: 38.8 us -> 42.1 us  [per_device(): lax.psum_scatter(partial_value, 'layer', scatter_dimension=0, tiled=True)]
  transfers between devices with their start and end apart: 3 -> 3, of which waited for: 3 -> 3; matrix products, arithmetic and copies ran while one was open for 2% -> 0% of each run, Pallas kernels for 0% -> 0%
where the time goes in v1:
time: 271 us; the launch traced here: 270 us
  waiting for transfers between devices  226 us (83%)
  between operations  13.4 us (5%)
  starting transfers between devices  11.4 us (4%)
  matrix products  10.1 us (4%)
  local copies, waits for them, and re-layouts  5.85 us (2%)
  other arithmetic  3.99 us (1%)
    all_to_all x1, waiting for transfers between devices, fit_the_pipes(): all_to_all(jnp.stack([here_x for _ in range(axis_size('col'))]), axis_nam...  140 us
    all_gather x1, waiting for transfers between devices, per_device(): gathered = lax.all_gather(slab_values, 'row', axis=0, tiled=True)  43.1 us
    reduce_scatter x1, waiting for transfers between devices, per_device(): lax.psum_scatter(partial_value, 'layer', scatter_dimension=0, tiled=True)  42.1 us
    all_to_all x1, starting transfers between devices, fit_the_pipes(): all_to_all(jnp.stack([here_x for _ in range(axis_size('col'))]), axis_nam...  11.3 us
    dot_general x1, matrix products, per_device(): jnp.dot(fit_the_pipes(1, masked), gathered, preferred_element_type=jnp.fl...  10.1 us
  transfers between devices with their start and end apart: 3, of which 3 were waited for; matrix products, arithmetic and copies ran while one was open for 0% of the time, Pallas kernels for 0%

profile of v1, /device:TPU:1, one launch (start us, length us, event | category | flops | bytes accessed | tf_op | source)
XLA Modules:
  0.0 270.4 jit_solution(9229839142298473458)
XLA Ops:
  6.5 0.7 convert_bitcast_fusion
  7.2 0.1 broadcast_bitcast_fusion
  7.3 1.4 broadcast_multiply_fusion
  8.6 0.2 copy.5
  8.9 4.3 %stack.3 = bf16[16,2048,128]{1,2,0:T(8,128)(2,1)} broadcast(bf16[2048,128]{0,1:T(8,128)(2,1)S(1)} %copy.5), dimensions={1,2} | broadcast | bytes 8912896 | tf_op jit(solution)/shard_map/stack | solution.py:12
  13.2 11.3 %all-to-all-start = ((bf16[16,2048,128]{1,2,0:T(8,128)(2,1)}), bf16[16,2048,128]{1,2,0:T(8,128)(2,1)}, u32[]{:S(2)}, u32[]{:S(2)}) async-start(bf16[16,2048,128]{1,2,0:T(8,128)(2,1)} %stack.3), calls=%async_computation | async-start | bytes 16777216 | tf_op jit(solution)/shard_map/all_to_all | solution.py:11
  24.5 0.0 all-gather.2.cloned.1.call-start
  24.6 0.7 all-gather.2.cloned.1.call-update
  25.3 0.0 reduce-scatter.2.cloned.1.call-start
  25.3 43.1 %all-gather.2.cloned.1.call-done = bf16[2048,384]{1,0:T(8,128)(2,1)} async-done(((bf16[256,384]{1,0:T(8,128)(2,1)}), bf16[2048,384]{1,0:T(8,128)(2,1)}) %all-gather.2.cloned.1.call-update) | async-done | bytes 1572880 | tf_op jit(solution)/shard_map/all_gather | solution.py:21
  68.4 139.7 %all-to-all-done = bf16[16,2048,128]{1,2,0:T(8,128)(2,1)} async-done(((bf16[16,2048,128]{1,2,0:T(8,128)(2,1)}), bf16[16,2048,128]{1,2,0:T(8,128)(2,1)}, u32[]{:S(2)}, u32[]{:S(2)}) %all-to-all-start) | async-done | bytes 8388640 | tf_op jit(solution)/shard_map/all_to_all | solution.py:11
  208.1 10.1 %fusion = f32[2048,384]{1,0:T(8,128)} fusion(bf16[2048,2048]{0,1:T(8,128)(2,1)} %bitcast.3, bf16[2048,384]{1,0:T(8,128)(2,1)} %all-gather.2.cloned.1.call-done), kind=kOutput, calls=%fused_computation.5 | convolution fusion | flops 3221225472 | bytes 13107200 | tf_op jit(solution)/shard_map/dot_general | solution.py:27
  218.2 0.0 copy-start
  218.2 0.0 reduce-scatter.2.cloned.1.call-update
  218.2 0.7 copy-done
  218.9 0.1 copy.6
  219.0 0.2 mul.29
  219.2 0.1 copy.10
  219.2 0.3 copy.7
  219.5 42.1 %reduce-scatter.2.cloned.1.call-done = f32[512,384]{1,0:T(8,128)} async-done(((f32[2048,384]{1,0:T(8,128)}), f32[512,384]{1,0:T(8,128)}) %reduce-scatter.2.cloned.1.call-update) | async-done | bytes 786448 | tf_op jit(solution)/shard_map/reduce_scatter | solution.py:28
  261.6 2.0 multiply_convert_fusion
  (1 shorter events, 0.0 us)
Async XLA Ops:
  13.2 194.9 %all-to-all-start = ((bf16[16,2048,128]{1,2,0:T(8,128)(2,1)}), bf16[16,2048,128]{1,2,0:T(8,128)(2,1)}, u32[]{:S(2)}, u32[]{:S(2)}) async-start(bf16[16,2048,128]{1,2,0:T(8,128)(2,1)} %stack.3), calls=%async_computation | async-start | bytes 16777216 | tf_op jit(solution)/shard_map/all_to_all | solution.py:11
  24.5 43.9 %all-gather.2.cloned.1.call-start = ((), (), s32[]{:S(2)}) async-start(), calls=%async_computation.2 | async-start | bytes 1769472 | tf_op jit(solution)/shard_map/all_gather | solution.py:21
  25.3 236.3 %reduce-scatter.2.cloned.1.call-start = ((), (), s32[]{:S(2)}) async-start(), calls=%async_computation.3 | async-start | bytes 3932160 | tf_op jit(solution)/shard_map/reduce_scatter | solution.py:28
  218.2 0.7 copy-start
Sparse Core Ops, SparseCore 0:
  27.4 40.9 all-gather.1
  218.4 43.2 reduce-scatter.1
